TPU v7x, 512 devices: a whole 4x8x8 slice. The times are simulated.
512 devices in a mesh: gx: 16 (over x, z_hi), gy: 32 (over z_lo, y, core).
Axes of the slice: x: 4, y: 8, z: 8 (z_hi: 4, z_lo: 2; z = z_hi * 2 + z_lo), core: 2. Of those that a mesh axis runs over, the one named last changes fastest.
Arguments:
- stem_tensor: float32 [512, 512, 512], P('gx', 'gy'), may hold values from -6 to 6
- branch_pool: float32 [8, 512, 512], P(None, 'gy'), may hold values from -0.25 to 0.25
- path_ids: int32 [4], replicated, may hold values from 0 to 7
- mode_orders: int32 [4, 9], replicated, may hold values from 0 to 8, each once within a row
Outputs:
- contracted: float32 [512, 512, 512], P('gx', 'gy')
All inputs are finite; a program needn't handle non-finite values.
Results may differ from a plain program's by a relative error of at most 0.00015.
Values sent between devices are 32-bit elements; how exact they have to be, the bound alone decides.
A program may use at most 64 MiB of HBM per device.

v0:
```python
import jax
import jax.numpy as jnp
from jax import lax
from jax.sharding import PartitionSpec as P


def row_order(mode_orders, step, extent):
    qubits = mode_orders.shape[1]
    index_of_row = jnp.arange(extent, dtype=jnp.int32)
    shift_list = jnp.arange(qubits, dtype=jnp.int32)
    bit_table = jnp.right_shift(index_of_row[:, None], shift_list[None, :]) & 1
    powers = jnp.left_shift(jnp.ones((qubits,), jnp.int32), mode_orders[step])
    return jnp.sum(bit_table * powers[None, :], axis=1)


def contract_branches(form, stem_array, branch_matrix):
    return jnp.einsum(
        form,
        stem_array,
        branch_matrix,
        precision=lax.Precision.HIGHEST,
        preferred_element_type=jnp.float32,
    )


def bring_b(stem_array):
    return lax.all_to_all(stem_array, "gy", split_axis=2, concat_axis=1, tiled=True)


def collect_first_operand(stem_array):
    return lax.all_to_all(stem_array, "gx", split_axis=2, concat_axis=0, tiled=True)


def on_device(stem_tensor, branch_pool, path_ids, mode_orders):
    extent = branch_pool.shape[2]

    def local_row_block(step):
        return lax.dynamic_index_in_dim(branch_pool, path_ids[step], 0, keepdims=False)

    def branch_lookup(step):
        whole = lax.all_gather(local_row_block(step), "gy", axis=0, tiled=True)
        return jnp.take(whole, row_order(mode_orders, step, extent), axis=0)

    stem_array = contract_branches("abc,cn->abn", stem_tensor, branch_lookup(0))
    stem_array = contract_branches("abc,bn->acn", bring_b(stem_array), branch_lookup(1))
    stem_array = contract_branches(
        "uej,uk->ejk", collect_first_operand(stem_array), branch_lookup(2)
    )
    regrouped = lax.all_to_all(stem_array, "gy", split_axis=2, concat_axis=0, tiled=True)
    stem_array = contract_branches("cba,cn->bna", regrouped, branch_lookup(3))
    result = lax.all_to_all(stem_array, "gy", split_axis=1, concat_axis=2, tiled=True)
    return result


def solution(mesh):
    placed = (P("gx", "gy", None), P(None, "gy", None), P(), P())
    return jax.shard_map(
        on_device, mesh=mesh, in_specs=placed, out_specs=P("gx", "gy", None), check_vma=False
    )
```

profile of v0, /device:TPU:1, one launch (start us, length us, event | category | flops | bytes accessed | tf_op | source)
XLA Modules:
  0.0 392.6 jit_solution(11950605822443286310)
XLA Ops:
  6.5 0.0 copy-start
  6.5 0.0 all-gather.11.cloned.1.call-start
  6.5 1.4 fusion.28
  15.5 1.5 constant_dynamic-slice_fusion.3
  17.0 0.0 all-gather.11.cloned.1.call-update
  17.0 0.0 all-gather.13.cloned.1.call-start
  17.1 0.7 all-gather.13.cloned.1.call-update
  17.8 0.8 shift-left_bitcast_fusion.3
  18.6 0.1 multiply_reduce_fusion.2
  18.7 70.6 %all-gather.11.cloned.1.call-done = f32[1,512,512]{2,1,0:T(8,128)} async-done(((f32[1,16,512]{2,1,0:T(8,128)}), f32[1,512,512]{2,1,0:T(8,128)}) %all-gather.11.cloned.1.call-update) | async-done | bytes 1048592 | tf_op jit(solution)/shard_map/all_gather | solution.py:41
  89.4 3.2 gather_fusion.1
  92.6 0.0 copy-done
  92.7 2.4 convolution_bitcast_fusion
  95.1 3.7 copy.50
  98.8 4.7 %reshape.57 = f32[32,1,8192]{2,1,0:T(1,128)} reshape(f32[512,16,32]{2,1,0:T(8,128)} %bitcast.67) | data formatting | bytes 2097152
  103.5 6.7 %all-to-all-start = ((f32[32,1,8192]{2,1,0:T(1,128)}), f32[32,1,8192]{2,1,0:T(1,128)S(1)}, u32[]{:S(2)}, u32[]{:S(2)}) async-start(f32[32,1,8192]{2,1,0:T(1,128)} %reshape.57), calls=%async_computation | async-start | bytes 2097152 | tf_op jit(solution)/shard_map/all_to_all | solution.py:27
  110.2 0.6 all-gather.15.cloned.1.call-start
  110.8 0.2 all-gather.15.cloned.1.call-update
  111.0 0.1 multiply_reduce_fusion.1
  111.1 51.5 %all-gather.13.cloned.1.call-done = f32[1,512,512]{2,1,0:T(8,128)} async-done(((f32[1,16,512]{2,1,0:T(8,128)}), f32[1,512,512]{2,1,0:T(8,128)}) %all-gather.13.cloned.1.call-update) | async-done | bytes 1048592 | tf_op jit(solution)/shard_map/all_gather | solution.py:41
  162.6 3.2 gather_fusion.2
  165.8 0.0 all-to-all-done
  165.9 0.5 broadcast.39
  166.4 3.2 reduce
  169.6 2.7 reshape.58
  172.3 5.9 %copy.52 = f32[32,32,16,16]{0,3,2,1:T(8,128)} copy(f32[32,32,16,16]{0,2,3,1:T(8,128)} %bitcast.71) | data formatting | bytes 2097152 | tf_op jit(solution)/shard_map/all_to_all | solution.py:27
  178.2 3.2 copy.53
  181.4 2.0 fusion.7
  183.5 3.8 copy.54
  187.3 4.7 %reshape.59 = f32[16,1,16384]{2,1,0:T(1,128)} reshape(f32[512,16,32]{2,1,0:T(8,128)} %bitcast.68) | data formatting | bytes 2097152
  192.0 8.7 %all-to-all-start.1 = ((f32[16,1,16384]{2,1,0:T(1,128)}), f32[16,1,16384]{2,1,0:T(1,128)S(1)}, u32[]{:S(2)}, u32[]{:S(2)}) async-start(f32[16,1,16384]{2,1,0:T(1,128)} %reshape.59), calls=%async_computation.1 | async-start | bytes 2097152 | tf_op jit(solution)/shard_map/all_to_all | solution.py:31
  200.7 0.2 all-gather.9.cloned.1.call-start
  200.9 0.4 all-gather.9.cloned.1.call-update
  201.3 0.1 multiply_reduce_fusion
  201.4 30.6 %all-gather.15.cloned.1.call-done = f32[1,512,512]{2,1,0:T(8,128)} async-done(((f32[1,16,512]{2,1,0:T(8,128)}), f32[1,512,512]{2,1,0:T(8,128)}) %all-gather.15.cloned.1.call-update) | async-done | bytes 1048592 | tf_op jit(solution)/shard_map/all_gather | solution.py:41
  232.0 3.2 gather_fusion.3
  235.3 0.0 all-to-all-done.1
  235.3 3.1 reduce.1
  238.4 2.7 reshape.60
  241.1 6.6 %copy.72 = f32[32,16,16,32]{0,2,3,1:T(8,128)} copy(f32[32,16,16,32]{0,1,3,2:T(8,128)} %bitcast.73) | data formatting | bytes 2097152 | tf_op jit(solution)/shard_map/all_to_all | solution.py:31
  247.7 3.5 all_to_all.59
  251.3 2.0 fusion.5
  253.3 3.7 copy.56
  256.9 4.7 %reshape.61 = f32[32,1,8192]{2,1,0:T(1,128)} reshape(f32[512,16,32]{2,1,0:T(8,128)} %bitcast.69) | data formatting | bytes 2097152
  261.7 10.1 %all-to-all-start.2 = ((f32[32,1,8192]{2,1,0:T(1,128)}), f32[32,1,8192]{2,1,0:T(1,128)S(1)}, u32[]{:S(2)}, u32[]{:S(2)}) async-start(f32[32,1,8192]{2,1,0:T(1,128)} %reshape.61), calls=%async_computation.2 | async-start | bytes 2097152 | tf_op jit(solution)/shard_map/all_to_all | solution.py:49
  271.8 0.1 multiply_reduce_fusion.3
  271.9 36.2 %all-gather.9.cloned.1.call-done = f32[1,512,512]{2,1,0:T(8,128)} async-done(((f32[1,16,512]{2,1,0:T(8,128)}), f32[1,512,512]{2,1,0:T(8,128)}) %all-gather.9.cloned.1.call-update) | async-done | bytes 1048592 | tf_op jit(solution)/shard_map/all_gather | solution.py:41
  308.0 3.2 gather_fusion
  311.3 0.0 all-to-all-done.2
  311.3 3.2 reduce.2
  314.5 2.7 reshape.62
  317.2 3.9 copy.58
  321.2 7.9 %fusion.2 = f32[32,512,16]{1,0,2:T(8,128)S(1)} fusion(f32[512,32,16]{1,2,0:T(8,128)S(1)} %bitcast.66, f32[512,512]{1,0:T(8,128)S(1)} %gather_fusion, pred[512]{0:T(512)(128)(4,1)S(1)} %compare_and_fusion.3), kind=kOutput, calls=%fused_computation.7 | convolution fusion | flops 1610874880 | bytes 3146240 | tf_op jit(solution)/shard_map/cba,cn->bna/dot_general | solution.py:17
  329.1 3.7 copy.60
  332.7 4.1 %reshape.63 = f32[32,1,8192]{2,1,0:T(1,128)S(1)} reshape(f32[512,16,32]{2,1,0:T(8,128)} %bitcast.70) | data formatting | bytes 2097152
  336.9 34.6 %all_to_all.72 = f32[32,1,8192]{2,1,0:T(1,128)S(1)} all-to-all(f32[32,1,8192]{2,1,0:T(1,128)S(1)} %reshape.63), channel_id=1, replica_groups=mesh['gx'=16,'gy'=32] {'gy'}, dimensions={0} | all-to-all | bytes 2097152 | tf_op jit(solution)/shard_map/all_to_all | solution.py:51
  371.5 3.2 reduce.3
  374.7 2.7 reshape.64
  377.4 0.0 copy-start.1
  377.4 4.7 %copy.61 = f32[32,16,32,16]{0,3,2,1:T(8,128)} copy(f32[32,16,32,16]{0,3,1,2:T(8,128)} %bitcast.76) | data formatting | bytes 2097152 | tf_op jit(solution)/shard_map/all_to_all | solution.py:51
  382.1 3.7 copy.62
  385.8 0.0 copy-done.1
  (12 shorter events, 0.1 us)
Async XLA Ops:
  6.5 86.1 %copy-start = (f32[32,16,512]{2,1,0:T(8,128)S(1)}, f32[32,16,512]{2,1,0:T(8,128)}, u32[]{:S(2)}) copy-start(f32[32,16,512]{2,1,0:T(8,128)} %param.6) | copy-start | bytes 3145732
  6.5 82.8 %all-gather.11.cloned.1.call-start = ((), (), s32[]{:S(2)}) async-start(), calls=%async_computation.5 | async-start | bytes 1081344 | tf_op jit(solution)/shard_map/all_gather | solution.py:41
  17.0 145.6 %all-gather.13.cloned.1.call-start = ((), (), s32[]{:S(2)}) async-start(), calls=%async_computation.6 | async-start | bytes 1081344 | tf_op jit(solution)/shard_map/all_gather | solution.py:41
  103.5 62.4 %all-to-all-start = ((f32[32,1,8192]{2,1,0:T(1,128)}), f32[32,1,8192]{2,1,0:T(1,128)S(1)}, u32[]{:S(2)}, u32[]{:S(2)}) async-start(f32[32,1,8192]{2,1,0:T(1,128)} %reshape.57), calls=%async_computation | async-start | bytes 2097152 | tf_op jit(solution)/shard_map/all_to_all | solution.py:27
  110.2 121.8 %all-gather.15.cloned.1.call-start = ((), (), s32[]{:S(2)}) async-start(), calls=%async_computation.7 | async-start | bytes 1081344 | tf_op jit(solution)/shard_map/all_gather | solution.py:41
  192.0 43.2 %all-to-all-start.1 = ((f32[16,1,16384]{2,1,0:T(1,128)}), f32[16,1,16384]{2,1,0:T(1,128)S(1)}, u32[]{:S(2)}, u32[]{:S(2)}) async-start(f32[16,1,16384]{2,1,0:T(1,128)} %reshape.59), calls=%async_computation.1 | async-start | bytes 2097152 | tf_op jit(solution)/shard_map/all_to_all | solution.py:31
  200.7 107.4 %all-gather.9.cloned.1.call-start = ((), (), s32[]{:S(2)}) async-start(), calls=%async_computation.4 | async-start | bytes 1081344 | tf_op jit(solution)/shard_map/all_gather | solution.py:41
  261.7 49.6 %all-to-all-start.2 = ((f32[32,1,8192]{2,1,0:T(1,128)}), f32[32,1,8192]{2,1,0:T(1,128)S(1)}, u32[]{:S(2)}, u32[]{:S(2)}) async-start(f32[32,1,8192]{2,1,0:T(1,128)} %reshape.61), calls=%async_computation.2 | async-start | bytes 2097152 | tf_op jit(solution)/shard_map/all_to_all | solution.py:49
  377.4 8.4 %copy-start.1 = (f32[32,16,512]{2,1,0:T(8,128)S(1)}, f32[32,16,512]{2,1,0:T(8,128)}, u32[]{:S(2)}) copy-start(f32[32,16,512]{2,1,0:T(8,128)} %param.6) | copy-start | bytes 3145732
Sparse Core Ops, SparseCore 0:
  17.1 72.1 all-gather.10
  91.5 71.0 all-gather.12
  164.7 67.2 all-gather.14
  234.0 73.9 all-gather.8
where the time goes:
time: 400 us; the launch traced here: 393 us
  waiting for transfers between devices  190 us (48%)
  local copies, waits for them, and re-layouts  91.9 us (23%)
  blocking collectives  34.6 us (9%)
  starting transfers between devices  26.3 us (7%)
  between operations  21.2 us (5%)
  matrix products  14.4 us (4%)
  other arithmetic  14 us (4%)
    all_gather x4, waiting for transfers between devices, branch_lookup(): whole = lax.all_gather(local_row_block(step), 'gy', axis=0, tiled=True)  189 us
    all_to_all x1, blocking collectives, on_device(): lax.all_to_all(stem_array, 'gy', split_axis=1, concat_axis=2, tiled=True)  34.6 us
    unnamed x12, local copies, waits for them, and re-layouts  29.1 us
    dot_general x4, matrix products, contract_branches(): jnp.einsum(form, stem_array, branch_matrix, precision=lax.Precision.HIGHE...  14.4 us
    gather x4, local copies, waits for them, and re-layouts, branch_lookup(): return jnp.take(whole, row_order(mode_orders, step, extent), axis=0)  13 us
    dot_general x3, local copies, waits for them, and re-layouts, contract_branches(): jnp.einsum(form, stem_array, branch_matrix, precision=lax.Precision.HIGHE...  11.2 us
    all_to_all x2, local copies, waits for them, and re-layouts, collect_first_operand(): lax.all_to_all(stem_array, 'gx', split_axis=2, concat_axis=0, tiled=True)  10.1 us
    all_to_all x1, starting transfers between devices, on_device(): lax.all_to_all(stem_array, 'gy', split_axis=2, concat_axis=0, tiled=True)  10.1 us
  transfers between devices with their start and end apart: 7, of which 4 were waited for; matrix products, arithmetic and copies ran while one was open for 19% of the time, Pallas kernels for 0%

commit v1 on v0

v1 whole, which is shorter than its diff:
```python
import functools

import jax
import jax.numpy as jnp
from jax import lax
from jax.experimental import pallas as pl
from jax.experimental.pallas import tpu as pltpu
from jax.sharding import PartitionSpec as P

MESH = pl.DeviceIdType.MESH
F32 = jnp.float32
BF16 = jnp.bfloat16
W = 512
QUBITS = 9
GX, GY = 16, 32


def halves(x):
    hi = x.astype(BF16)
    return hi, (x - hi.astype(F32)).astype(BF16)


def dot(a, b, dims=((1,), (0,))):
    return lax.dot_general(a, b, (dims, ((), ())), preferred_element_type=F32)


def dot3(a, b):
    return dot(a[0], b[0]) + (dot(a[0], b[1]) + dot(a[1], b[0]))


def swap_blocks(rows):
    lane = lax.broadcasted_iota(jnp.int32, (16, 128), 1)
    rows = list(rows)
    for t in (4, 2, 1):
        low = (lane // (16 * t)) % 2 == 0
        for u in range(8):
            if u & t == 0:
                a, b = rows[u], rows[u + t]
                rows[u] = jnp.where(low, a, pltpu.roll(b, 16 * t, 1))
                rows[u + t] = jnp.where(low, pltpu.roll(a, 128 - 16 * t, 1), b)
    return rows


def kernel(
    stem, pool, path, modes, out,
    sel, bf, xa, b1_hi, b1_lo, b03_hi, b03_lo, b2_hi, b2_lo, tmp, z, s, r,
    pool_sem, own_sem, s_own, r_own, s_y, r_y, s_z, r_z, s_a, r_a, s_f, r_f, s_c, r_c, s_x, r_x, s_o, r_o, all_in,
):
    gx, gy = lax.axis_index("gx"), lax.axis_index("gy")
    x, zh = gx // 4, gx % 4
    zl, y, core = gy // 16, (gy // 2) % 8, gy % 2
    zz = zh * 2 + zl

    def device(x_, y_, z_, core_):
        return {"gx": x_ * 4 + z_ // 2, "gy": (z_ % 2) * 16 + y_ * 2 + core_}

    def send(src, dst, s_sem, r_sem, to):
        pltpu.make_async_remote_copy(
            src_ref=src, dst_ref=dst, send_sem=s_sem, recv_sem=r_sem, device_id=to, device_id_type=MESH
        ).start()

    def wait(ref, sem):
        pltpu.make_async_copy(ref, ref, sem).wait()

    barrier = pltpu.get_barrier_semaphore()
    greeted = [{"gy": (gy + d) % GY} for d in range(1, GY)] + [{"gx": (gx + d) % GX} for d in range(1, GX)]
    for to in greeted:
        pl.semaphore_signal(barrier, inc=1, device_id=to, device_id_type=MESH)
    for h in range(1, 4):
        pl.semaphore_signal(
            barrier, inc=1, device_id={"gx": x * 4 + (zh + h) % 4, "gy": (gy + 16) % GY}, device_id_type=MESH
        )

    own = pltpu.make_async_copy(stem.at[gy], xa.at[pl.ds(0, 16)], own_sem)
    own.start()
    chosen = [
        pltpu.make_async_copy(pool, sel, pool_sem),
    ]
    for c in chosen:
        c.start()
    for c in chosen:
        c.wait()
    lanes_x = pl.ds(pl.multiple_of(x * 128, 128), 128)
    mine = y % 4 == zh
    y_hi = y // 4
    half = pl.multiple_of(core * 256, 256)
    part = pl.multiple_of(half + zz * 32, 32)
    picked = [sel[path[k]] for k in range(4)]
    for k in range(4):
        tmp[pl.ds(16 * k, 16), :] = picked[k]

    pl.semaphore_wait(barrier, (GY - 1) + (GX - 1) + 3)
    for d in range(1, GX):
        pl.semaphore_signal(all_in, inc=1, device_id={"gx": (gx + d) % GX}, device_id_type=MESH)

    own_rows = pl.ds(pl.multiple_of(part + y_hi * 16, 16), 16)

    @pl.when(mine)
    def _():
        for k in range(4):
            bf[k, own_rows, lanes_x] = tmp[pl.ds(16 * k, 16), lanes_x]
        for d in range(1, 8):
            send(bf.at[:, own_rows, lanes_x], bf.at[:, own_rows, lanes_x], s_y, r_y.at[y_hi], device(x, (y + d) % 8, zz, core))

    for d in range(1, GY):
        send(stem.at[(gy + d) % GY], xa.at[pl.ds(16 * d, 16)], s_x, r_x.at[d // 8], {"gy": (gy + d) % GY})

    for yy in range(2):
        @pl.when(jnp.logical_not(jnp.logical_and(mine, y_hi == yy)))
        def _():
            wait(bf.at[:, pl.ds(0, 16), pl.ds(0, 128)], r_y.at[yy])

    order = (0, 3, 1, 2)

    def send_z(k):
        block = bf.at[k, pl.ds(part, 32), lanes_x]
        for d in range(1, 8):
            send(block, block, s_z, r_z.at[k], device(x, y, (zz + d) % 8, core))

    def send_x(k):
        wait(bf.at[k, pl.ds(0, 224), pl.ds(0, 128)], r_z.at[k])
        block = bf.at[k, pl.ds(half, 256), lanes_x]
        for way, d in ((0, 1), (1, 3)):
            send(block, block, s_a, r_a.at[k, way], device((x + d) % 4, y, zz, core))

    def forward_x(k):
        for way, d in ((0, 1), (1, 3)):
            wait(bf.at[k, pl.ds(0, 256), pl.ds(0, 128)], r_a.at[k, way])
            lanes = pl.ds(pl.multiple_of(((x + 4 - d) % 4) * 128, 128), 128)
            block = bf.at[k, pl.ds(pl.multiple_of(half + 128 * way, 128), 128), lanes]
            send(block, block, s_f, r_f.at[k, way], device((x + d) % 4, y, zz, core))

    def send_c(k):
        for way in range(2):
            wait(bf.at[k, pl.ds(0, 128), pl.ds(0, 128)], r_f.at[k, way])
        block = bf.at[k, pl.ds(half, 256)]
        send(block, block, s_c, r_c.at[k], {"gy": gy + 1 - 2 * core})

    def whole(k):
        wait(bf.at[k, pl.ds(0, 256)], r_c.at[k])

    def source_row(k, row):
        q = jnp.zeros_like(row)
        for t in range(QUBITS):
            q = q + ((row >> t) & 1) * (jnp.int32(1) << modes[k, t])
        return q

    at = lax.broadcasted_iota(jnp.int32, (1, W), 1)
    z_at = (at // 32) % 8
    held_row = ((z_at % 2) * 16 + (z_at // 2 + 4 * ((at // 16) % 2)) * 2 + at // 256) * 16 + at % 16

    def permuted(k, row):
        pick = jnp.where(source_row(k, row) == held_row, 1.0, 0.0).astype(BF16)
        hi, lo = halves(bf[k])
        return dot(pick, hi), dot(pick, lo)

    t = lax.broadcasted_iota(jnp.int32, (W, 1), 0)

    for k in order:
        send_z(k)
    send_x(0)
    send_x(3)
    send_x(1)
    forward_x(0)
    forward_x(3)
    send_c(0)
    forward_x(1)
    send_c(3)
    send_x(2)
    whole(0)
    hi, lo = permuted(0, t)
    b1_hi[...] = hi.astype(BF16)
    b1_lo[...] = lo.astype(BF16)
    send_c(1)
    forward_x(2)
    whole(3)
    hi, lo = permuted(3, t)
    turn = (W - 16 * gy) % W
    hi = pltpu.roll(hi, turn, 1).astype(BF16)
    lo = pltpu.roll(lo, turn, 1).astype(BF16)
    b03 = dot3((b1_hi[...], b1_lo[...]), (hi, lo))
    hi, lo = halves(b03)
    b03_hi[...] = hi
    b03_lo[...] = lo

    whole(1)
    hi, lo = permuted(1, ((gy + GY - t // 16) % GY) * 16 + t % 16)
    m_at = (t % 16) * 32 + t // 16
    swap = jnp.where(m_at == at, 1.0, 0.0).astype(BF16)
    b1_hi[...] = dot(swap, hi.astype(BF16), ((1,), (1,))).astype(BF16)
    b1_lo[...] = dot(swap, lo.astype(BF16), ((1,), (1,))).astype(BF16)

    own.wait()
    w = []
    for g in range(4):
        rows = 7 if g == 0 else 8
        wait(xa.at[pl.ds(0, 16 * rows)], r_x.at[g])
        xg = halves(xa[pl.ds(128 * g, 128), :])
        w = halves(dot3(xg, (b03_hi[...], b03_lo[...])))
        if g < 3:
            b1 = (b1_hi[:, pl.ds(128 * g, 128)], b1_lo[:, pl.ds(128 * g, 128)])
            if g == 0:
                z[...] = dot3(b1, w)
            else:
                z[...] += dot3(b1, w)

    pl.semaphore_wait(all_in, GX - 1)
    b1 = (b1_hi[:, pl.ds(384, 128)], b1_lo[:, pl.ds(384, 128)])
    for j in range(4):
        cols = slice(128 * j, 128 * j + 128)
        zj = z[:, cols] + dot3(b1, (w[0][:, cols], w[1][:, cols]))
        for m in range(4):
            turned = swap_blocks([zj[16 * (8 * m + u):16 * (8 * m + u) + 16] for u in range(8)])
            for v in range(8):
                s[pl.ds(128 * j + 16 * v, 16), pl.ds(128 * m, 128)] = turned[v]

        def row_group(jj, first, j=j):
            jrel = 8 * j + jj
            to_y = (gy + jrel) % GY
            for irel in range(first, GX):
                to_x = (gx + irel) % GX
                send(s.at[pl.ds(jrel * 16 + to_x, 1)], r.at[pl.ds(jrel * 16 + irel, 1)], s_o, r_o.at[j], {"gx": to_x, "gy": to_y})

        if j == 0:
            pltpu.make_async_copy(s.at[pl.ds(gx, 1)], r.at[pl.ds(0, 1)], r_o.at[0]).start()
            row_group(0, 1)

        def body(jj, carry, row_group=row_group):
            row_group(jj, 0)
            return carry

        lax.fori_loop(1 if j == 0 else 0, 8, body, 0)

    send_c(2)
    whole(2)
    hi, lo = permuted(2, ((gx + GX - t % 16) % GX) * 32 + (gy + GY - t // 16) % GY)
    b2_hi[...] = hi.astype(BF16)
    b2_lo[...] = lo.astype(BF16)

    for j in range(4):
        wait(r.at[pl.ds(0, 128)], r_o.at[j])
        rows = pl.ds(128 * j, 128)
        rj = halves(jnp.transpose(r[rows, :]))
        term = dot3(rj, (b2_hi[rows, :], b2_lo[rows, :]))
        if j == 0:
            out[...] = term
        else:
            out[...] += term

    @pl.when(mine)
    def _():
        wait(bf.at[:, pl.ds(0, 112), pl.ds(0, 128)], s_y)
    wait(bf.at[:, pl.ds(0, 224), pl.ds(0, 128)], s_z)
    wait(bf.at[0], s_a)
    wait(bf.at[0, pl.ds(0, 256)], s_f)
    wait(bf.at[pl.ds(0, 2)], s_c)
    wait(xa.at[pl.ds(0, 496)], s_x)
    wait(r.at[pl.ds(0, 504)], s_o)
    for e in range(7):
        wait(r.at[pl.ds(e, 1)], s_o)


def on_device(stem, pool, path, modes):
    any_space = pl.BlockSpec(memory_space=pl.ANY)
    smem = pl.BlockSpec(memory_space=pltpu.SMEM)
    square = pltpu.VMEM((W, W), F32)
    piece = pltpu.VMEM((W, W), BF16)
    dma = pltpu.SemaphoreType.DMA
    result = pl.pallas_call(
        kernel,
        out_shape=jax.ShapeDtypeStruct((W, W), F32),
        in_specs=[any_space, any_space, smem, smem],
        out_specs=pl.BlockSpec(memory_space=pltpu.VMEM),
        scratch_shapes=[
            pltpu.VMEM((8, 16, W), F32), pltpu.VMEM((4, W, W), F32), square,
            piece, piece, piece, piece, piece, piece,
            pltpu.VMEM((64, W), F32), square, square, square,
            dma, dma, dma, dma,
            dma, dma((2,)), dma, dma((4,)), dma, dma((4, 2)), dma, dma((4, 2)), dma, dma((4,)),
            dma, dma((4,)), dma, dma((4,)), pltpu.SemaphoreType.REGULAR,
        ],
        compiler_params=pltpu.CompilerParams(collective_id=0, has_side_effects=True, vmem_limit_bytes=48 << 20),
    )(stem, pool, path, modes)
    return result.reshape(32, 16, W)


def solution(mesh):
    return jax.shard_map(
        on_device,
        mesh=mesh,
        in_specs=(P("gx", "gy", None), P(None, "gy", None), P(), P()),
        out_specs=P("gx", "gy", None),
        check_vma=False,
    )
```

time: 400 us -> 97.9 us (0.24); the launches traced: 393 us -> 97.7 us
  waiting for transfers between devices: 190 us -> 0 us
  Pallas kernels: 0 us -> 93.2 us
  local copies, waits for them, and re-layouts: 91.9 us -> 4.48 us
  blocking collectives: 34.6 us -> 0 us
  starting transfers between devices: 26.3 us -> 0 us
  between operations: 21.2 us -> 0.01 us
  matrix products: 14.4 us -> 0 us
  other arithmetic: 14 us -> 0 us
    all_gather x4 -> x0, waiting for transfers between devices: 189 us -> none  [branch_lookup(): whole = lax.all_gather(local_row_block(step), 'gy', axis=0, tiled=True)]
    pallas_call x0 -> x1, Pallas kernels: none -> 93.2 us  [on_device(): pl.pallas_call(kernel, out_shape=jax.ShapeDtypeStruct((W, W), F32), in_sp...]
    all_to_all x1 -> x0, blocking collectives: 34.6 us -> none  [on_device(): lax.all_to_all(stem_array, 'gy', split_axis=1, concat_axis=2, tiled=True)]
    all_to_all x8 -> x0, local copies, waits for them, and re-layouts: 32.1 us -> none  [the longest x2 10.1 us: collect_first_operand(): lax.all_to_all(stem_array, 'gx', split_axis=2, concat_axis=0, tiled=True)]
    all_to_all x3 -> x0, starting transfers between devices: 25.5 us -> none  [the longest x1 10.1 us: on_device(): lax.all_to_all(stem_array, 'gy', split_axis=2, concat_axis=0, tiled=True)]
    unnamed x12 -> x9, local copies, waits for them, and re-layouts: 29.1 us -> 4.48 us
    dot_general x4 -> x0, matrix products: 14.4 us -> none  [contract_branches(): jnp.einsum(form, stem_array, branch_matrix, precision=lax.Precision.HIGHE...]
    gather x4 -> x0, local copies, waits for them, and re-layouts: 13 us -> none  [branch_lookup(): return jnp.take(whole, row_order(mode_orders, step, extent), axis=0)]
  transfers between devices with their start and end apart: 7 -> 0, of which waited for: 4 -> 0; matrix products, arithmetic and copies ran while one was open for 19% -> 0% of each run, Pallas kernels for 0% -> 0%
where the time goes in v1:
time: 97.9 us; the launch traced here: 97.7 us
  Pallas kernels  93.2 us (95%)
  local copies, waits for them, and re-layouts  4.48 us (5%)
    pallas_call x1, Pallas kernels, on_device(): pl.pallas_call(kernel, out_shape=jax.ShapeDtypeStruct((W, W), F32), in_sp...  93.2 us
    unnamed x9, local copies, waits for them, and re-layouts  4.48 us

profile of v1, /device:TPU:1, one launch (start us, length us, event | category | flops | bytes accessed | tf_op | source)
XLA Modules:
  0.0 97.7 jit_solution(2309109429993773735)
XLA Ops:
  0.0 0.0 copy-start
  0.0 1.2 %copy-done = f32[32,16,512]{2,1,0:T(8,128)S(1)} copy-done((f32[32,16,512]{2,1,0:T(8,128)S(1)}, f32[32,16,512]{2,1,0:T(8,128)}, u32[]{:S(2)}) %copy-start) | copy-done | bytes 1048600
  1.2 0.0 copy-start.1
  1.2 0.9 copy-done.1
  2.2 0.0 copy-start.2
  2.2 0.7 copy-done.2
  2.9 0.0 copy-start.3
  2.9 0.7 copy-done.3
  3.5 93.2 %shard_map.46 = f32[512,512]{1,0:T(8,128)S(1)} custom-call(f32[32,16,512]{2,1,0:T(8,128)S(1)} %copy-done, f32[8,16,512]{2,1,0:T(8,128)S(1)} %copy-done.1, s32[4]{0:T(128)S(1)} %copy-done.3, s32[4,9]{1,0:T(4,128)S(1)} %copy-done.2), custom_call_target="tpu_custom_call" | custom-call | tf_op jit(solution)/shard_map/pallas_call | solution.py:269
  96.7 1.0 copy.6
Async XLA Ops:
  0.0 1.2 %copy-start = (f32[32,16,512]{2,1,0:T(8,128)S(1)}, f32[32,16,512]{2,1,0:T(8,128)}, u32[]{:S(2)}) copy-start(f32[32,16,512]{2,1,0:T(8,128)} %stem.1) | copy-start | bytes 3145732
  1.2 0.9 copy-start.1
  2.2 0.7 copy-start.2
  2.9 0.7 copy-start.3

commit v2 on v1

v2 whole, which is shorter than its diff:
```python
import functools

import jax
import jax.numpy as jnp
from jax import lax
from jax.experimental import pallas as pl
from jax.experimental.pallas import tpu as pltpu
from jax.sharding import PartitionSpec as P

MESH = pl.DeviceIdType.MESH
F32 = jnp.float32
BF16 = jnp.bfloat16
W = 512
VMEM = 62 << 20
QUBITS = 9
GX, GY = 16, 32
FIRST = ((0,), (0,))
PACE = (8, 0, 8, 8, 8)


def halves(x):
    hi = x.astype(BF16)
    return hi, (x - hi.astype(F32)).astype(BF16)


def dot(a, b, dims=((1,), (0,))):
    return lax.dot_general(a, b, (dims, ((), ())), preferred_element_type=F32)


def dot3(a, b, dims=((1,), (0,))):
    return dot(a[0], b[0], dims) + (dot(a[0], b[1], dims) + dot(a[1], b[0], dims))


def swap_blocks(rows):
    lane = lax.broadcasted_iota(jnp.int32, (16, 128), 1)
    rows = list(rows)
    for t in (4, 2, 1):
        low = (lane // (16 * t)) % 2 == 0
        for u in range(8):
            if u & t == 0:
                a, b = rows[u], rows[u + t]
                rows[u] = jnp.where(low, a, pltpu.roll(b, 16 * t, 1))
                rows[u + t] = jnp.where(low, pltpu.roll(a, 128 - 16 * t, 1), b)
    return rows


def kernel(
    stem, pool, path_in, modes_in, out,
    path, modes, sel, bf, xa, pick, p_hi, p_lo, q_hi, q_lo, z, s, r,
    in_sem, own_sem, s_y, r_y, s_z, r_z, s_a, r_a, s_f, r_f, s_c, r_c, s_x, r_x, s_o, r_o, all_in,
):
    gx, gy = lax.axis_index("gx"), lax.axis_index("gy")
    x, zh = gx // 4, gx % 4
    zl, y, core = gy // 16, (gy // 2) % 8, gy % 2
    zz = zh * 2 + zl

    def device(x_, y_, z_, core_):
        return {"gx": x_ * 4 + z_ // 2, "gy": (z_ % 2) * 16 + y_ * 2 + core_}

    def send(src, dst, s_sem, r_sem, to):
        pltpu.make_async_remote_copy(
            src_ref=src, dst_ref=dst, send_sem=s_sem, recv_sem=r_sem, device_id=to, device_id_type=MESH
        ).start()

    def wait(ref, sem):
        pltpu.make_async_copy(ref, ref, sem).wait()

    barrier = pltpu.get_barrier_semaphore()
    greeted = [{"gy": (gy + d) % GY} for d in range(1, GY)] + [{"gx": (gx + d) % GX} for d in range(1, GX)]
    greeted += [{"gx": x * 4 + (zh + h) % 4, "gy": (gy + 16) % GY} for h in range(1, 4)]
    for to in greeted:
        pl.semaphore_signal(barrier, inc=1, device_id=to, device_id_type=MESH)

    own = pltpu.make_async_copy(stem.at[gy], xa.at[pl.ds(0, 16)], own_sem)
    taken = [
        pltpu.make_async_copy(pool, sel, in_sem.at[0]),
        pltpu.make_async_copy(path_in, path, in_sem.at[1]),
        pltpu.make_async_copy(modes_in, modes, in_sem.at[2]),
    ]
    for c in taken:
        c.start()
    own.start()
    for c in taken:
        c.wait()

    lanes_x = pl.ds(pl.multiple_of(x * 128, 128), 128)
    mine = y % 4 == zh
    y_hi = y // 4
    half = pl.multiple_of(core * 256, 256)
    part = pl.multiple_of(half + zz * 32, 32)
    own_rows = pl.ds(pl.multiple_of(part + y_hi * 16, 16), 16)

    @pl.when(mine)
    def _():
        for k in range(4):
            bf[k, own_rows, lanes_x] = sel[path[k], :, lanes_x]

    pl.semaphore_wait(barrier, len(greeted))

    @pl.when(mine)
    def _():
        for d in range(1, 8):
            send(bf.at[:, own_rows, lanes_x], bf.at[:, own_rows, lanes_x], s_y, r_y.at[y_hi], device(x, (y + d) % 8, zz, core))

    left = list(range(1, GY))
    pace = list(PACE)

    def some_stem(count=0):
        for _ in range(count or (pace.pop(0) if pace else 0)):
            if left:
                d = left.pop(0)
                send(stem.at[(gy + d) % GY], xa.at[pl.ds(16 * d, 16)], s_x, r_x, {"gy": (gy + d) % GY})

    some_stem()
    for d in range(1, GX):
        pl.semaphore_signal(all_in, inc=1, device_id={"gx": (gx + d) % GX}, device_id_type=MESH)

    t = lax.broadcasted_iota(jnp.int32, (W, 1), 0)
    at = lax.broadcasted_iota(jnp.int32, (1, W), 1)
    z_at = (at // 32) % 8
    held_row = ((z_at % 2) * 16 + (z_at // 2 + 4 * ((at // 16) % 2)) * 2 + at // 256) * 16 + at % 16

    def make_pick(k, row):
        q = jnp.zeros_like(row)
        for b in range(QUBITS):
            q = q + ((row >> b) & 1) * (jnp.int32(1) << modes[k, b])
        pick[k] = jnp.where(q == held_row, 1.0, 0.0).astype(BF16)

    make_pick(0, t)
    make_pick(3, t)

    for yy in range(2):
        @pl.when(jnp.logical_not(jnp.logical_and(mine, y_hi == yy)))
        def _():
            wait(bf.at[:, pl.ds(0, 16), pl.ds(0, 128)], r_y.at[yy])

    def send_z(k):
        block = bf.at[k, pl.ds(part, 32), lanes_x]
        for d in (1, 7, 2, 6, 3, 5, 4):
            send(block, block, s_z, r_z.at[k], device(x, y, (zz + d) % 8, core))

    def send_x(k):
        wait(bf.at[k, pl.ds(0, 224), pl.ds(0, 128)], r_z.at[k])
        block = bf.at[k, pl.ds(half, 256), lanes_x]
        for way, d in ((0, 1), (1, 3)):
            send(block, block, s_a, r_a.at[k, way], device((x + d) % 4, y, zz, core))

    def forward_x(k):
        for way, d in ((0, 1), (1, 3)):
            wait(bf.at[k, pl.ds(0, 256), pl.ds(0, 128)], r_a.at[k, way])
            lanes = pl.ds(pl.multiple_of(((x + 4 - d) % 4) * 128, 128), 128)
            block = bf.at[k, pl.ds(pl.multiple_of(half + 128 * way, 128), 128), lanes]
            send(block, block, s_f, r_f.at[k, way], device((x + d) % 4, y, zz, core))

    def send_c(k):
        for way in range(2):
            wait(bf.at[k, pl.ds(0, 128), pl.ds(0, 128)], r_f.at[k, way])
        block = bf.at[k, pl.ds(half, 256)]
        send(block, block, s_c, r_c.at[k], {"gy": gy + 1 - 2 * core})

    def whole(k):
        wait(bf.at[k, pl.ds(0, 256)], r_c.at[k])
        return halves(bf[k])

    for k in (0, 3, 1):
        send_z(k)
    some_stem()
    make_pick(1, ((gy + GY - t // 16) % GY) * 16 + t % 16)
    make_pick(2, ((gx + GX - t % 16) % GX) * 32 + ((gy // 8 + 4 - t // 128) % 4) * 8 + (t // 16) % 8)
    for k in (0, 3, 1):
        send_x(k)
        some_stem()
    send_z(2)
    forward_x(0)
    some_stem()
    forward_x(3)
    some_stem()
    send_c(0)
    forward_x(1)
    some_stem(GY)
    send_x(2)
    send_c(3)

    hi, lo = whole(0)
    hi, lo = dot(pick[0], hi).astype(BF16), dot(pick[0], lo).astype(BF16)
    p_hi[...] = dot(hi, pick[3]).astype(BF16)
    p_lo[...] = dot(lo, pick[3]).astype(BF16)
    send_c(1)

    b03 = dot3((p_hi[...], p_lo[...]), whole(3))
    p_hi[...], p_lo[...] = halves(b03)

    own.wait()
    wait(xa.at[pl.ds(0, 496)], r_x)
    hi, lo = halves(dot3(halves(xa[...]), (p_hi[...], p_lo[...])))
    q_hi[...] = dot(pick[1], hi, FIRST).astype(BF16)
    q_lo[...] = dot(pick[1], lo, FIRST).astype(BF16)

    forward_x(2)
    p_hi[...], p_lo[...] = whole(1)
    pl.semaphore_wait(all_in, GX - 1)
    for c in range(4):
        to_high = (gy // 8 + c) % 4
        cols = pl.ds(pl.multiple_of(to_high * 128, 128), 128)
        z[...] = dot3((p_hi[...], p_lo[...]), (q_hi[:, cols], q_lo[:, cols]), FIRST)
        for m in range(4):
            turned = swap_blocks([z[pl.ds(8 * m + u, 16, stride=32), :] for u in range(8)])
            for v in range(8):
                s[pl.ds(128 * c + 16 * v, 16), pl.ds(128 * m, 128)] = turned[v]

        def row_group(jj, first, c=c, to_high=to_high):
            low = (gy + jj) % 8
            src = 128 * c + low * 16
            dst = 128 * c + (gy % 8) * 16
            for i in range(first, GX):
                to_x = (gx + i) % GX
                send(s.at[pl.ds(src + to_x, 1)], r.at[pl.ds(dst + i, 1)], s_o, r_o.at[c], {"gx": to_x, "gy": to_high * 8 + low})

        if c == 0:
            own_row = (gy % 8) * 16
            pltpu.make_async_copy(s.at[pl.ds(own_row + gx, 1)], r.at[pl.ds(own_row, 1)], r_o.at[0]).start()
            row_group(0, 1)

        def body(jj, carry, row_group=row_group):
            row_group(jj, 0)
            return carry

        lax.fori_loop(1 if c == 0 else 0, 8, body, 0)

    send_c(2)
    hi, lo = whole(2)
    q_hi[...] = dot(pick[2], hi).astype(BF16)
    q_lo[...] = dot(pick[2], lo).astype(BF16)

    for c in range(4):
        wait(r.at[pl.ds(0, 128)], r_o.at[c])
        rows = pl.ds(128 * c, 128)
        term = dot3(halves(r[rows, :]), (q_hi[rows, :], q_lo[rows, :]), FIRST)
        if c == 0:
            out[...] = term
        else:
            out[...] += term

    @pl.when(mine)
    def _():
        wait(bf.at[:, pl.ds(0, 112), pl.ds(0, 128)], s_y)
    wait(bf.at[:, pl.ds(0, 224), pl.ds(0, 128)], s_z)
    wait(bf.at[0], s_a)
    wait(bf.at[0, pl.ds(0, 256)], s_f)
    wait(bf.at[pl.ds(0, 2)], s_c)
    wait(xa.at[pl.ds(0, 496)], s_x)
    wait(r.at[pl.ds(0, 504)], s_o)
    for e in range(7):
        wait(r.at[pl.ds(e, 1)], s_o)


def on_device(stem, pool, path, modes):
    hbm = pl.BlockSpec(memory_space=pltpu.HBM)
    square = pltpu.VMEM((W, W), F32)
    piece = pltpu.VMEM((W, W), BF16)
    dma = pltpu.SemaphoreType.DMA
    result = pl.pallas_call(
        kernel,
        out_shape=jax.ShapeDtypeStruct((W, W), F32),
        in_specs=[hbm, hbm, hbm, hbm],
        out_specs=pl.BlockSpec(memory_space=pltpu.VMEM),
        scratch_shapes=[
            pltpu.SMEM((4,), jnp.int32), pltpu.SMEM((4, QUBITS), jnp.int32),
            pltpu.VMEM((8, 16, W), F32), pltpu.VMEM((4, W, W), F32), square,
            pltpu.VMEM((4, W, W), BF16), piece, piece, piece, piece,
            pltpu.VMEM((W, 128), F32), square, square,
            dma((3,)), dma,
            dma, dma((2,)), dma, dma((4,)), dma, dma((4, 2)), dma, dma((4, 2)), dma, dma((4,)),
            dma, dma, dma, dma((4,)), pltpu.SemaphoreType.REGULAR,
        ],
        compiler_params=pltpu.CompilerParams(collective_id=0, has_side_effects=True, vmem_limit_bytes=VMEM),
    )(stem, pool, path, modes)
    return result.reshape(32, 16, W)


def solution(mesh):
    return jax.shard_map(
        on_device,
        mesh=mesh,
        in_specs=(P("gx", "gy", None), P(None, "gy", None), P(), P()),
        out_specs=P("gx", "gy", None),
        check_vma=False,
    )
```

time: 97.9 us -> 90.4 us (0.923)
  the two profiles are of different devices: /device:TPU:1 before, /device:TPU:17 now
where the time goes in v2:
time: 90.4 us; the launch traced here: 90.3 us
  Pallas kernels  88 us (97%)
  local copies, waits for them, and re-layouts  2.31 us (3%)
    pallas_call x1, Pallas kernels, on_device(): pl.pallas_call(kernel, out_shape=jax.ShapeDtypeStruct((W, W), F32), in_sp...  88 us
    unnamed x1, local copies, waits for them, and re-layouts  2.31 us

profile of v2, /device:TPU:17, one launch (start us, length us, event | category | flops | bytes accessed | tf_op | source)
XLA Modules:
  0.0 90.3 jit_solution(11311211189928083928)
XLA Ops:
  0.0 88.0 %shard_map.46 = f32[512,512]{1,0:T(8,128)} custom-call(f32[32,16,512]{2,1,0:T(8,128)} %stem.1, f32[8,16,512]{2,1,0:T(8,128)} %pool.1, s32[4]{0:T(128)} %path_in.1, s32[4,9]{1,0:T(4,128)} %modes_in.1), custom_call_target="tpu_custom_call" | custom-call | tf_op jit(solution)/shard_map/pallas_call | solution.py:262
  88.0 2.3 %copy.6 = f32[32,16,512]{2,1,0:T(8,128)} copy(f32[32,16,512]{2,1,0:T(8,128)} %bitcast.1) | data formatting | bytes 2097152

commit v3 on v2

--- a/solution.py
+++ b/solution.py
@@ -15,7 +15,7 @@
 QUBITS = 9
 GX, GY = 16, 32
 FIRST = ((0,), (0,))
-PACE = (8, 0, 8, 8, 8)
+PACE = (16, 0, 6, 6, 3)
 
 
 def halves(x):
@@ -139,11 +139,16 @@
         for d in (1, 7, 2, 6, 3, 5, 4):
             send(block, block, s_z, r_z.at[k], device(x, y, (zz + d) % 8, core))
 
+    def send_c(k, d):
+        block = bf.at[k, pl.ds(half, 256), pl.ds(pl.multiple_of(((x + d) % 4) * 128, 128), 128)]
+        send(block, block, s_c, r_c.at[k], {"gy": gy + 1 - 2 * core})
+
     def send_x(k):
         wait(bf.at[k, pl.ds(0, 224), pl.ds(0, 128)], r_z.at[k])
         block = bf.at[k, pl.ds(half, 256), lanes_x]
         for way, d in ((0, 1), (1, 3)):
             send(block, block, s_a, r_a.at[k, way], device((x + d) % 4, y, zz, core))
+        send_c(k, 0)
 
     def forward_x(k):
         for way, d in ((0, 1), (1, 3)):
@@ -151,12 +156,13 @@
             lanes = pl.ds(pl.multiple_of(((x + 4 - d) % 4) * 128, 128), 128)
             block = bf.at[k, pl.ds(pl.multiple_of(half + 128 * way, 128), 128), lanes]
             send(block, block, s_f, r_f.at[k, way], device((x + d) % 4, y, zz, core))
-
-    def send_c(k):
+        for d in (1, 3):
+            send_c(k, d)
+
+    def finish_x(k):
         for way in range(2):
             wait(bf.at[k, pl.ds(0, 128), pl.ds(0, 128)], r_f.at[k, way])
-        block = bf.at[k, pl.ds(half, 256)]
-        send(block, block, s_c, r_c.at[k], {"gy": gy + 1 - 2 * core})
+        send_c(k, 2)
 
     def whole(k):
         wait(bf.at[k, pl.ds(0, 256)], r_c.at[k])
@@ -175,17 +181,17 @@
     some_stem()
     forward_x(3)
     some_stem()
-    send_c(0)
+    finish_x(0)
     forward_x(1)
     some_stem(GY)
     send_x(2)
-    send_c(3)
+    finish_x(3)
 
     hi, lo = whole(0)
     hi, lo = dot(pick[0], hi).astype(BF16), dot(pick[0], lo).astype(BF16)
     p_hi[...] = dot(hi, pick[3]).astype(BF16)
     p_lo[...] = dot(lo, pick[3]).astype(BF16)
-    send_c(1)
+    finish_x(1)
 
     b03 = dot3((p_hi[...], p_lo[...]), whole(3))
     p_hi[...], p_lo[...] = halves(b03)
@@ -227,7 +233,7 @@
 
         lax.fori_loop(1 if c == 0 else 0, 8, body, 0)
 
-    send_c(2)
+    finish_x(2)
     hi, lo = whole(2)
     q_hi[...] = dot(pick[2], hi).astype(BF16)
     q_lo[...] = dot(pick[2], lo).astype(BF16)

time: 90.4 us -> 89.3 us (0.988)
  the two profiles are of different devices: /device:TPU:17 before, /device:TPU:1 now
where the time goes in v3:
time: 89.3 us; the launch traced here: 89.1 us
  Pallas kernels  86.8 us (97%)
  local copies, waits for them, and re-layouts  2.31 us (3%)
    pallas_call x1, Pallas kernels, on_device(): pl.pallas_call(kernel, out_shape=jax.ShapeDtypeStruct((W, W), F32), in_sp...  86.8 us
    unnamed x1, local copies, waits for them, and re-layouts  2.31 us

profile of v3, /device:TPU:1, one launch (start us, length us, event | category | flops | bytes accessed | tf_op | source)
XLA Modules:
  0.0 89.1 jit_solution(9556670663024559298)
XLA Ops:
  0.0 86.8 %shard_map.46 = f32[512,512]{1,0:T(8,128)} custom-call(f32[32,16,512]{2,1,0:T(8,128)} %stem.1, f32[8,16,512]{2,1,0:T(8,128)} %pool.1, s32[4]{0:T(128)} %path_in.1, s32[4,9]{1,0:T(4,128)} %modes_in.1), custom_call_target="tpu_custom_call" | custom-call | tf_op jit(solution)/shard_map/pallas_call | solution.py:268
  86.8 2.3 %copy.6 = f32[32,16,512]{2,1,0:T(8,128)} copy(f32[32,16,512]{2,1,0:T(8,128)} %bitcast.1) | data formatting | bytes 2097152
